TPU v7x, 256 devices: a whole 4x4x8 slice. The times are simulated.
256 devices in a mesh: grp: 2 (over z_hi), fsdp: 128 (over z_lo, y, x, core).
Axes of the slice: x: 4, y: 4, z: 8 (z_hi: 2, z_lo: 4; z = z_hi * 4 + z_lo), core: 2. Of those that a mesh axis runs over, the one named last changes fastest.
Arguments:
- hidden_act: bfloat16 [131072, 1024], P(('grp', 'fsdp')), may hold values from -24 to 24
- out_grad: bfloat16 [131072, 1024], P(('grp', 'fsdp')), may hold values from -0.015625 to 0.015625
- layer_stats: float32 [4096, 512], P(('grp', 'fsdp')), may hold values from -4 to 4
- resident_stats: float32 [1024, 512, 512], P(('grp', 'fsdp')), as said below
- slot_block: int32 [1024], replicated, may hold values from 0 to 1023, as said below
- layer_refresh: int32 [64], replicated, may hold values from 0 to 1, as said below
Outputs:
- grad_shard: float32 [1024, 1024], P(('grp', 'fsdp'))
- stats_new: float32 [4096, 512], P(('grp', 'fsdp'))
- pair_roots: float32 [256, 512, 512], P(('grp', 'fsdp'))
Inputs may be any that keep to these rules, and one draw needn't show every extreme that they name: slot_block is a permutation of the 1024 block numbers; block b belongs to layer b // 16; for every fsdp index the 8 slots of its two devices (one of each group) hold exactly two blocks whose layer is refreshed; at some fsdp index both lie on the device of group 0, at some other both on the device of group 1. `layer_refresh`: a quarter of the 64 layers are 1. `resident_stats`: every block is symmetric positive definite.
All inputs are finite; a program needn't handle non-finite values.
Results may differ from a plain program's by a relative error of at most 0.0003.
Values sent between devices are 32-bit elements; how exact they have to be, the bound alone decides.
A program may use at most 64 MiB of HBM per device.

v0:
```python
import jax
import jax.numpy as jnp
from jax import lax
from jax.sharding import PartitionSpec as P

BPL = 16
ITERS = 3


EPSILON = 0.0001
HIGHEST = lax.Precision.HIGHEST


def partner_2(value, axis, stride):
    return lax.ppermute(value, axis, [(i, i ^ 1 << stride) for i in range(lax.axis_size(axis))])


def fourth_root(stat):
    identity = jnp.eye(stat.shape[-1], dtype=stat.dtype)
    matrix = stat + EPSILON * identity
    magnitude = jnp.sqrt(jnp.sum(matrix * matrix, axis=(-2, -1), keepdims=True) + 1e-06)
    scaling = 2.5 / magnitude
    moving = scaling * matrix
    iterate = jnp.sqrt(jnp.sqrt(scaling)) * identity
    for number in range(ITERS):
        factor = (5.0 * identity - moving) * 0.25
        iterate = jnp.matmul(iterate, factor, precision=HIGHEST)
        square = jnp.matmul(factor, factor, precision=HIGHEST)
        fourth = jnp.matmul(square, square, precision=HIGHEST)
        moving = jnp.matmul(fourth, moving, precision=HIGHEST)
    return iterate


def ranked_pick(marks, wanted):
    places = jnp.arange(marks.shape[0], dtype=jnp.int32)
    ranks = jnp.cumsum(marks, dtype=jnp.int32) - 1
    return jnp.sum(places * marks * (ranks == wanted).astype(jnp.int32), dtype=jnp.int32)


def on_device(hidden_act, out_grad, layer_stats, resident_stats, slot_block, layer_refresh):
    groups = lax.axis_size("grp")
    shards = lax.axis_size("fsdp")
    group = lax.axis_index("grp")
    shard = lax.axis_index("fsdp")
    row_width = hidden_act.shape[1]
    col_width = out_grad.shape[1]
    block_size = resident_stats.shape[1]
    slot_count = resident_stats.shape[0]
    contract = (((0,), (0,)), ((), ()))
    stat_rows = layer_stats.shape[0]
    device = group * shards + shard
    first_row = device * stat_rows
    which = first_row // block_size
    inner = first_row % block_size
    tile_index = which // 2
    tiles_across = col_width // block_size
    row_start = tile_index // tiles_across * block_size
    col_start = tile_index % tiles_across * block_size
    grad_shard = lax.psum_scatter(
        lax.dot_general(hidden_act, out_grad, contract, preferred_element_type=jnp.float32),
        ("grp", "fsdp"),
        scatter_dimension=0,
        tiled=True,
    )
    section = lax.all_gather(grad_shard, "fsdp", axis=0, tiled=True)
    local_start = row_start - group * (row_width // groups)
    block = lax.dynamic_slice(section, (local_start, col_start), (block_size, block_size))
    lead_rows = lax.dynamic_slice_in_dim(block, inner, stat_rows, 0)
    left_part = jnp.dot(lead_rows, block.T, precision=HIGHEST) / block_size
    lead_cols = lax.dynamic_slice_in_dim(block, inner, stat_rows, 1)
    right_part = jnp.dot(lead_cols.T, block, precision=HIGHEST) / block_size
    stats_new = layer_stats + jnp.where(which % 2 == 0, left_part, right_part)
    layers = layer_refresh.shape[0]
    layer_of = slot_block // BPL
    table = (layer_of[:, None] == jnp.arange(layers, dtype=jnp.int32)[None, :]).astype(jnp.int32)
    flags = jnp.sum(table * layer_refresh[None, :], axis=1, dtype=jnp.int32)
    lower_flags = lax.dynamic_slice_in_dim(flags, shard * slot_count, slot_count)
    upper_flags = lax.dynamic_slice_in_dim(flags, (shards + shard) * slot_count, slot_count)
    lower_count = jnp.sum(lower_flags, dtype=jnp.int32)
    own_flags = jnp.where(group == 0, lower_flags, upper_flags)
    picks = jnp.stack([ranked_pick(own_flags, 0), ranked_pick(own_flags, 1)])
    picked = jnp.take(resident_stats, picks, axis=0)
    roots = fourth_root(picked)
    partner = partner_2(roots, "grp", 0)
    lower_roots = jnp.where(group == 0, roots, partner)
    upper_roots = jnp.where(group == 0, partner, roots)
    first_root = jnp.where(lower_count >= 1, lower_roots[0], upper_roots[0])
    second_root = jnp.where(
        lower_count >= 2,
        lower_roots[1],
        jnp.where(lower_count == 1, upper_roots[0], upper_roots[1]),
    )
    pair_roots = jnp.where(group == 0, first_root, second_root)[None]
    return (grad_shard, stats_new, pair_roots)


def solution(mesh):
    in_specs = (
        P(("grp", "fsdp"), None),
        P(("grp", "fsdp"), None),
        P(("grp", "fsdp"), None),
        P(("grp", "fsdp"), None, None),
        P(),
        P(),
    )
    out_specs = (P(("grp", "fsdp"), None), P(("grp", "fsdp"), None), P(("grp", "fsdp"), None, None))
    return jax.shard_map(
        on_device, mesh=mesh, in_specs=in_specs, out_specs=out_specs, check_vma=False
    )
```

profile of v0, /device:TPU:1, one launch (start us, length us, event | category | flops | bytes accessed | tf_op | source)
XLA Modules:
  0.0 581.0 jit_solution(9114491725598236166)
XLA Ops:
  7.2 0.0 copy-start
  7.2 0.0 all-reduce.3.cloned.1.call-start
  7.2 1.2 copy-done
  8.4 4.5 fusion.60
  12.9 0.0 all-reduce.3.cloned.1.call-update
  12.9 0.0 copy-start.10
  12.9 0.0 copy-start.11
  12.9 0.0 all-gather.3.cloned.1.call-start
  13.0 1.6 fusion.32
  14.6 0.0 copy-done.10
  14.6 0.1 select_reduce_fusion
  14.8 0.7 dynamic-slice_reduce_fusion
  15.5 0.2 reduce-window.9
  15.6 0.6 fusion.47
  16.3 1.3 fusion.49
  17.5 1.3 compare_and_fusion
  18.8 2.9 gather_fusion
  21.7 0.0 copy-start.1
  21.7 0.0 copy-start.6
  21.7 1.9 multiply_reduce_fusion
  23.7 5.7 fusion.9
  29.3 5.8 %fusion.61 = f32[2,512,512]{2,1,0:T(8,128)S(1)} fusion(f32[2,512,512]{2,1,0:T(8,128)} %fusion.9), kind=kOutput, calls=%fused_computation.92 | convolution fusion | flops 3221225472 | bytes 4194304 | tf_op jit(solution)/shard_map/dot_general | solution.py:29
  35.2 0.0 copy-done.7
  35.2 0.0 copy-start.2
  35.2 3.9 fusion.5
  39.1 3.9 fusion.7
  43.1 3.5 fusion.62
  46.6 4.8 fusion.63
  51.5 232.8 %all-reduce.3.cloned.1.call-done = f32[1024,1024]{1,0:T(8,128)} async-done(((f32[1024,1024]{1,0:T(8,128)}), f32[1024,1024]{1,0:T(8,128)}) %all-reduce.3.cloned.1.call-update) | async-done | bytes 4194320
  284.3 1.4 fusion.75
  285.6 0.0 all-gather.3.cloned.1.call-update
  285.7 0.1 fusion.33
  285.8 0.0 copy-start.3
  285.8 5.7 fusion.3
  291.8 0.0 copy-done.5
  291.8 0.0 copy-start.8
  291.8 3.7 fusion.8
  295.5 0.0 copy-done.8
  295.5 3.7 fusion
  299.2 4.8 collective-permute-start
  306.0 1.4 constant_dynamic-slice_fusion
  307.3 90.7 %collective-permute-done = f32[2,512,512]{2,1,0:T(8,128)} collective-permute-done((f32[2,512,512]{2,1,0:T(8,128)S(1)}, f32[2,512,512]{2,1,0:T(8,128)}, u32[]{:S(2)}, u32[]{:S(2)}) %collective-permute-start) | collective-permute-done | bytes 2097184 | tf_op jit(solution)/shard_map/ppermute | solution.py:15
  398.1 2.3 broadcast_select_fusion.1
  400.4 1.5 fusion.13
  401.9 168.0 %all-gather.3.cloned.1.call-done = f32[128,4,1024]{2,1,0:T(4,128)} async-done(((f32[1,4,1024]{2,1,0:T(4,128)}), f32[128,4,1024]{2,1,0:T(4,128)}) %all-gather.3.cloned.1.call-update) | async-done | bytes 2097168 | tf_op jit(solution)/shard_map/all_gather | solution.py:65
  569.9 2.0 reshape.177
  571.9 0.7 convolution_multiply_fusion.1
  572.6 1.6 fusion.11
  (14 shorter events, 0.1 us)
Async XLA Ops:
  7.2 1.2 copy-start
  7.2 277.1 %all-reduce.3.cloned.1.call-start = ((), (), s32[]{:S(2)}) async-start(), calls=%async_computation.1 | async-start | bytes 8388608
  12.9 1.7 copy-start.10
  12.9 1.7 copy-start.11
  12.9 556.9 %all-gather.3.cloned.1.call-start = ((), (), s32[]{:S(2)}) async-start(), calls=%async_computation | async-start | bytes 2113536 | tf_op jit(solution)/shard_map/all_gather | solution.py:65
  21.7 2.0 copy-start.1
  21.7 1.9 copy-start.6
  29.3 5.8 %copy-start.7 = (f32[512,512]{1,0:T(8,128)S(1)}, f32[512,512]{1,0:T(8,128)}, u32[]{:S(2)}) copy-start(f32[512,512]{1,0:T(8,128)} %get-tuple-element.12) | copy-start | bytes 3145732
  35.2 3.9 copy-start.2
  39.1 7.5 %copy-start.4 = (f32[2,512,512]{2,1,0:T(8,128)}, f32[2,512,512]{2,1,0:T(8,128)S(1)}, u32[]{:S(2)}) copy-start(f32[2,512,512]{2,1,0:T(8,128)S(1)} %fusion.5) | copy-start | bytes 6291460
  285.8 5.8 copy-start.3
  285.8 6.0 %copy-start.5 = (f32[2,512,512]{2,1,0:T(8,128)S(1)}, f32[2,512,512]{2,1,0:T(8,128)}, u32[]{:S(2)}) copy-start(f32[2,512,512]{2,1,0:T(8,128)} %copy-done.4) | copy-start | bytes 6291460
  291.8 3.7 copy-start.8
  299.2 98.9 %collective-permute-start = (f32[2,512,512]{2,1,0:T(8,128)S(1)}, f32[2,512,512]{2,1,0:T(8,128)}, u32[]{:S(2)}, u32[]{:S(2)}) collective-permute-start(f32[2,512,512]{2,1,0:T(8,128)S(1)} %fusion), channel_id=1, source_target_pairs={{0,128},{128,0},{1,129},{129,1},{2,130},{130,2},{3,131},{131,3},{4... | collective-permute-start | bytes 6291464 | tf_op jit(solution)/shard_map/ppermute | solution.py:15
  401.9 170.7 %copy-start.9 = (f32[16,512]{1,0:T(8,128)S(1)}, f32[16,512]{1,0:T(8,128)}, u32[]{:S(2)}) copy-start(f32[16,512]{1,0:T(8,128)} %param.8) | copy-start | bytes 98308
Sparse Core Ops, SparseCore 0:
  13.5 270.7 all-reduce.2
  286.9 282.9 all-gather.2
where the time goes:
time: 581 us
  waiting for transfers between devices  492 us (85%)
  matrix products  47.6 us (8%)
  between operations  16.5 us (3%)
  other arithmetic  11.6 us (2%)
  local copies, waits for them, and re-layouts  8.82 us (2%)
    unnamed x3, waiting for transfers between devices  233 us
    all_gather x1, waiting for transfers between devices, on_device(): section = lax.all_gather(grad_shard, 'fsdp', axis=0, tiled=True)  168 us
    ppermute x1, waiting for transfers between devices, partner_2(): lax.ppermute(value, axis, [(i, i ^ 1 << stride) for i in range(lax.axis_s...  90.7 us
    dot_general x3, matrix products, fourth_root(): iterate = jnp.matmul(iterate, factor, precision=HIGHEST)  13.1 us
  transfers between devices with their start and end apart: 3, of which 3 were waited for; matrix products, arithmetic and copies ran while one was open for 10% of the time, Pallas kernels for 0%

commit v1 on v0

v1 whole, which is shorter than its diff:
```python
import jax
import jax.numpy as jnp
from jax import lax
from jax.experimental import pallas as pl
from jax.experimental.pallas import tpu as pltpu
from jax.sharding import PartitionSpec as P

BPL = 16
EPSILON = 0.0001
MESH = pl.DeviceIdType.MESH
F32 = jnp.float32
BF16 = jnp.bfloat16
ZL, NY, NX, NZ = 4, 4, 4, 8
BLK = 512
HALF = 256
ROWS = 256


def split(value):
    high = value.astype(BF16)
    return high, (value - high.astype(F32)).astype(BF16)


def dot(a, b, dims=(((1,), (0,)), ((), ()))):
    return lax.dot_general(a, b, dims, preferred_element_type=F32)


def kernel(
    hid_any, og_any, stats_in, res_any, slot_block, refresh,
    grad_out, stats_out, root_out,
    hid, og, res, g_send, g_own, core_recv, p1a, p1b, a1, b1, p2a, p2b, r, p3, fin, fin_other,
    tile, t_high, t_low, wide, pack, pack_recv,
    m0, m0_h, m0_l, q_h, q_l, r_h, r_l, w_h, w_l, p_f, p_h, p_l,
    in_sem, send_sem, recv_sem,
):
    grp = lax.axis_index("grp")
    f = lax.axis_index("fsdp")
    zl = f // 32
    y = (f // 8) % NY
    x = (f // 2) % NX
    c = f % 2
    z = grp * ZL + zl
    active = c == zl // 2

    def dev(z_, y_, x_, c_):
        return (z_ // ZL, (z_ % ZL) * 32 + y_ * 8 + x_ * 2 + c_)

    partner = dev(z, y, x, 1 - c)
    xs = [dev(z, y, (x + k) % NX, c) for k in range(1, NX)]
    ys = [dev(z, (y + k) % NY, x, c) for k in range(1, NY)]
    zs = [dev((z + k) % NZ, y, x, c) for k in range(1, NZ)]

    sends = iter(range(100))
    recvs = iter(range(100))

    def copy(src, dst, to, recv=None):
        s = send_sem.at[next(sends)]
        return pltpu.make_async_remote_copy(
            src_ref=src, dst_ref=dst, send_sem=s,
            recv_sem=recv_sem.at[next(recvs)] if recv is None else recv,
            device_id=to, device_id_type=MESH,
        )

    loads = [
        pltpu.make_async_copy(src, dst, in_sem.at[i])
        for i, (src, dst) in enumerate([(og_any, og), (hid_any, hid), (res_any, res)])
    ]
    for load in loads:
        load.start()
    barrier = pltpu.get_barrier_semaphore()
    peers = [partner] + xs + ys + zs
    for peer in peers:
        pl.semaphore_signal(barrier, inc=1, device_id=peer, device_id_type=MESH)

    own = (grp * 128 + f) * 4
    flags = [refresh[slot_block[own + l] // BPL] for l in range(4)]
    count = flags[0] + flags[1] + flags[2] + flags[3]
    pick0 = jnp.int32(0)
    pick1 = jnp.int32(0)
    before = jnp.int32(0)
    for l in range(4):
        pick0 = pick0 + jnp.where(before == 0, flags[l], 0) * l
        pick1 = pick1 + jnp.where(before == 1, flags[l], 0) * l
        before = before + flags[l]
    send_pick = jnp.where(grp == 0, pick1, pick0)
    own_pick = jnp.where(jnp.logical_and(grp == 1, count == 2), pick1, pick0)
    use_recv = count == 0

    def grad_part(dst, half):
        columns = pl.ds(pl.multiple_of(half * BLK, BLK), BLK)

        def step(i, carry):
            rows = pl.ds(pl.multiple_of(i * ROWS, ROWS), ROWS)
            part = dot(hid[:, rows], og[:, columns], (((0,), (0,)), ((), ())))
            dst[pl.ds(i * 2, 2)] = part.reshape(2, NY, NX, 8, BLK)
            return carry

        lax.fori_loop(0, 1024 // ROWS, step, 0)

    loads[0].wait()
    loads[1].wait()
    grad_part(g_send, 1 - c)

    loads[2].wait()
    row = lax.broadcasted_iota(jnp.int32, (HALF, HALF), 0)
    col = lax.broadcasted_iota(jnp.int32, (HALF, HALF), 1)
    lower_block = res[send_pick, HALF:, HALF:]
    pack[0:HALF] = res[send_pick, :HALF, HALF:]
    pack[HALF:2 * HALF] = jnp.where(row <= col, res[send_pick, :HALF, :HALF], lower_block)
    diagonal = jnp.sum(jnp.where(row == col, lower_block, 0.0), axis=0, keepdims=True)
    pack[2 * HALF:2 * HALF + 8] = jnp.broadcast_to(diagonal, (8, HALF))

    pl.semaphore_wait(barrier, len(peers))

    core = [copy(g_send.at[pl.ds(4 * i, 4)], core_recv.at[pl.ds(4 * i, 4)], partner) for i in range(2)]
    for item in core:
        item.start()
    exchange = copy(pack, pack_recv, zs[3])
    exchange.start()
    grad_part(g_own, c)

    phase1 = []
    for i, (axis_peers, buf) in enumerate(((xs, p1a), (ys, p1b))):
        core[i].wait_recv()

        def add(j, carry, i=i):
            g_own[4 * i + j] += core_recv[4 * i + j]
            return carry

        lax.fori_loop(0, 4, add, 0)
        group = []
        for k in range(1, 4):
            src = g_own.at[pl.ds(0, 4), :, (x + k) % NX] if i == 0 else g_own.at[pl.ds(4, 4), (y + k) % NY]
            group.append(copy(src, buf.at[k - 1], axis_peers[k - 1]))
            group[-1].start()
        phase1.append(group)
    phase2 = []
    for i, (axis_peers, buf, got, total) in enumerate(((ys, p2a, p1a, a1), (xs, p2b, p1b, b1))):
        for item in phase1[i]:
            item.wait_recv()

        def add(j, carry, i=i, got=got, total=total):
            mine = g_own[j, :, x] if i == 0 else g_own[4 + j, y]
            total[j] = mine + got[0, j] + got[1, j] + got[2, j]
            return carry

        lax.fori_loop(0, 4, add, 0)
        group = []
        for k in range(1, 4):
            at = (y + k) % NY if i == 0 else (x + k) % NX
            group.append(copy(total.at[:, at], buf.at[k - 1], axis_peers[k - 1]))
            group[-1].start()
        phase2.append(group)
    for i, (got, total, at) in enumerate(((p2a, a1, y), (p2b, b1, x))):
        for item in phase2[i]:
            item.wait_recv()
        r[4 * i:4 * i + 4] = total[:, at] + got[0] + got[1] + got[2]
    phase3 = []
    for k in range(1, NZ):
        phase3.append(copy(r.at[(z + k) % NZ], p3.at[k - 1], zs[k - 1]))
        phase3[-1].start()
    for item in phase3:
        item.wait_recv()
    mine = r[z]
    for k in range(7):
        mine = mine + p3[k]
    fin[...] = mine

    swap = copy(fin, fin_other, partner)
    swap.start()

    gz_base = [next(recvs) for _ in range(4)][0]
    gz = []
    for t in range(2):
        to = 2 * c + t
        item = copy(
            fin, tile.at[zl, y, x], dev(grp * ZL + to, y, x, c), recv_sem.at[gz_base + zl]
        )
        pl.when(to != zl)(item.start)
        gz.append((to != zl, item))

    def gather_z():
        tile[zl, y, x] = mine
        for k in range(1, 4):
            source = (zl + k) % ZL
            pltpu.make_async_remote_copy(
                src_ref=fin, dst_ref=tile.at[source, y, x], send_sem=send_sem.at[0],
                recv_sem=recv_sem.at[gz_base + source], device_id=partner, device_id_type=MESH,
            ).wait_recv()

    pl.when(active)(gather_z)

    def pair(k, i, stage):
        if stage == 1:
            return (tile.at[pl.ds(0, 2), y, x], ys[k - 1]) if i == 0 else (tile.at[pl.ds(2, 2), y, x], xs[k - 1])
        return (tile.at[pl.ds(0, 2), :, x], xs[k - 1]) if i == 0 else (tile.at[pl.ds(2, 2), y], ys[k - 1])

    stages = []
    for stage in (1, 2):
        stages.append([[copy(*(lambda s, d: (s, s, d))(*pair(k, i, stage))) for k in range(1, 4)] for i in range(2)])
    slabs = [
        [tile.at[pl.ds(0, 2), :, (x + 4 - k) % NX] for k in range(4)],
        [tile.at[pl.ds(2, 2), (y + 4 - k) % NY] for k in range(4)],
    ]
    forward = [[copy(slabs[i][k], slabs[i][k], partner) for k in range(4)] for i in range(2)]

    def gather_plane():
        for group in stages[0]:
            for item in group:
                item.start()
        for i in range(2):
            for k, item in enumerate(stages[0][i]):
                item.wait_recv()
            for item in stages[1][i]:
                item.start()
            forward[i][0].start()
        for k in range(1, 4):
            for i in range(2):
                stages[1][i][k - 1].wait_recv()
                forward[i][k].start()
        for stage in stages:
            for group in stage:
                for item in group:
                    item.wait_send()
        for group in forward:
            for item in group:
                item.wait_send()

    pl.when(active)(gather_plane)

    def take_forward():
        for i in range(2):
            for k in range(4):
                forward[i][k].wait_recv()

    pl.when(jnp.logical_not(active))(take_forward)

    swap.wait_recv()
    low = jnp.where(c == 0, fin[...], fin_other[...])
    high = jnp.where(c == 0, fin_other[...], fin[...])
    grad_out[:, :BLK] = jnp.where(c == 0, low[:4], low[4:])
    grad_out[:, BLK:] = jnp.where(c == 0, high[:4], high[4:])

    t_value = tile[...].reshape(BLK, BLK)
    t_h, t_l = split(t_value)
    t_high[...] = t_h
    t_low[...] = t_l
    at = (f % 32) * 16

    def left():
        dims = (((1,), (1,)), ((), ()))
        rows = pl.ds(pl.multiple_of(at, 16), 16)
        lead_h, lead_l = t_high[rows, :], t_low[rows, :]
        part = dot(lead_h, t_high[...], dims) + dot(lead_h, t_low[...], dims) + dot(lead_l, t_high[...], dims)
        stats_out[...] = stats_in[...] + part * (1.0 / BLK)

    def right():
        dims = (((0,), (0,)), ((), ()))
        columns = pl.ds(pl.multiple_of(at // 128 * 128, 128), 128)
        lead_h, lead_l = t_high[:, columns], t_low[:, columns]
        wide[...] = dot(lead_h, t_high[...], dims) + dot(lead_h, t_low[...], dims) + dot(lead_l, t_high[...], dims)
        part = wide[pl.ds(pl.multiple_of(at % 128, 16), 16), :]
        stats_out[...] = stats_in[...] + part * (1.0 / BLK)

    pl.when(zl % 2 == 0)(left)
    pl.when(zl % 2 == 1)(right)

    exchange.wait_recv()
    eye = (row == col).astype(F32)
    upper = pack_recv[HALF:2 * HALF]
    flipped = upper.T
    off = pack_recv[0:HALF]
    block_a = jnp.where(row <= col, upper, flipped)
    block_d = jnp.where(row > col, upper, flipped)
    block_d = jnp.where(row == col, jnp.broadcast_to(pack_recv[2 * HALF:2 * HALF + 1], (HALF, HALF)), block_d)
    total = jnp.zeros((1, 1), F32)
    for i, j, got in ((0, 0, block_a), (0, 1, off), (1, 0, off.T), (1, 1, block_d)):
        rows, cols = pl.ds(i * HALF, HALF), pl.ds(j * HALF, HALF)
        value = jnp.where(use_recv, got, res[own_pick, rows, cols])
        if i == j:
            value = value + EPSILON * eye
        m0[rows, cols] = value
        total = total + jnp.sum(value * value, axis=(0, 1), keepdims=True)
    zeta = 2.5 / jnp.sqrt(total + 1e-06)
    scale = jnp.sqrt(jnp.sqrt(zeta))

    def blocks(body):
        def step(i, carry):
            body(i, pl.ds(pl.multiple_of(i * ROWS, ROWS), ROWS))
            return carry
        lax.fori_loop(0, BLK // ROWS, step, 0)

    def put(high, low, rows, value):
        value_h, value_l = split(value)
        high[rows, :] = value_h
        low[rows, :] = value_l

    def product(ah, al, bh, bl, rows):
        lead = ah[rows, :]
        return dot(lead, bh[...]) + dot(lead, bl[...]) + dot(al[rows, :], bh[...])

    def ident(i):
        r_ = lax.broadcasted_iota(jnp.int32, (ROWS, BLK), 0) + i * ROWS
        c_ = lax.broadcasted_iota(jnp.int32, (ROWS, BLK), 1)
        return (r_ == c_).astype(F32)

    def step0(i, rows):
        value = m0[rows, :] * zeta
        m0[rows, :] = value
        put(m0_h, m0_l, rows, value)

    def step1(i, rows):
        square = product(m0_h, m0_l, m0_h, m0_l, rows)
        m = m0[rows, :]
        put(w_h, w_l, rows, (5.0 * m - square) * 0.25)
        put(q_h, q_l, rows, (25.0 * ident(i) - 10.0 * m + square) * 0.0625)

    def step2(i, rows):
        put(r_h, r_l, rows, product(q_h, q_l, q_h, q_l, rows))

    def step3(i, rows):
        fifth = product(r_h, r_l, w_h, w_l, rows)
        factor = (5.0 * ident(i) - m0[rows, :]) * 0.25
        value = (5.0 * factor - fifth) * 0.25
        p_f[rows, :] = value
        put(p_h, p_l, rows, value)

    def step4(i, rows):
        put(q_h, q_l, rows, product(p_h, p_l, p_h, p_l, rows))

    def step5(i, rows):
        put(w_h, w_l, rows, product(p_h, p_l, m0_h, m0_l, rows))

    def step6(i, rows):
        fifth = product(r_h, r_l, w_h, w_l, rows)
        root_out[0, rows, :] = (5.0 * p_f[rows, :] - fifth) * (0.25 * scale)

    for body in (step0, step1, step2, step3, step4, step5, step2, step6):
        blocks(body)

    for item in core + [exchange, swap] + phase1[0] + phase1[1] + phase2[0] + phase2[1] + phase3:
        item.wait_send()
    for sent, item in gz:
        pl.when(sent)(item.wait_send)


def on_device(hidden_act, out_grad, layer_stats, resident_stats, slot_block, layer_refresh):
    vmem = pl.BlockSpec(memory_space=pltpu.VMEM)
    anywhere = pl.BlockSpec(memory_space=pl.ANY)
    smem = pl.BlockSpec(memory_space=pltpu.SMEM)
    square = (BLK, BLK)
    piece = (8, BLK)
    scratch = [
        pltpu.VMEM(hidden_act.shape, BF16),
        pltpu.VMEM(out_grad.shape, BF16),
        pltpu.VMEM(resident_stats.shape, F32),
        pltpu.VMEM((NZ, NY, NX) + piece, F32),
        pltpu.VMEM((NZ, NY, NX) + piece, F32),
        pltpu.VMEM((NZ, NY, NX) + piece, F32),
        pltpu.VMEM((3, 4, NY) + piece, F32),
        pltpu.VMEM((3, 4, NX) + piece, F32),
        pltpu.VMEM((4, NY) + piece, F32),
        pltpu.VMEM((4, NX) + piece, F32),
        pltpu.VMEM((3, 4) + piece, F32),
        pltpu.VMEM((3, 4) + piece, F32),
        pltpu.VMEM((NZ,) + piece, F32),
        pltpu.VMEM((7,) + piece, F32),
        pltpu.VMEM(piece, F32),
        pltpu.VMEM(piece, F32),
        pltpu.VMEM((ZL, NY, NX) + piece, F32),
        pltpu.VMEM(square, BF16),
        pltpu.VMEM(square, BF16),
        pltpu.VMEM((128, BLK), F32),
        pltpu.VMEM((2 * HALF + 8, HALF), F32),
        pltpu.VMEM((2 * HALF + 8, HALF), F32),
        pltpu.VMEM(square, F32),
        pltpu.VMEM(square, BF16),
        pltpu.VMEM(square, BF16),
        pltpu.VMEM(square, BF16),
        pltpu.VMEM(square, BF16),
        pltpu.VMEM(square, BF16),
        pltpu.VMEM(square, BF16),
        pltpu.VMEM(square, BF16),
        pltpu.VMEM(square, BF16),
        pltpu.VMEM(square, F32),
        pltpu.VMEM(square, BF16),
        pltpu.VMEM(square, BF16),
        pltpu.SemaphoreType.DMA((3,)),
        pltpu.SemaphoreType.DMA((64,)),
        pltpu.SemaphoreType.DMA((64,)),
    ]
    return pl.pallas_call(
        kernel,
        out_shape=(
            jax.ShapeDtypeStruct((4, 1024), F32),
            jax.ShapeDtypeStruct(layer_stats.shape, F32),
            jax.ShapeDtypeStruct((1, BLK, BLK), F32),
        ),
        in_specs=[anywhere, anywhere, vmem, anywhere, smem, smem],
        out_specs=(vmem, vmem, vmem),
        scratch_shapes=scratch,
        compiler_params=pltpu.CompilerParams(
            collective_id=0, has_side_effects=True, vmem_limit_bytes=48 * 1024 * 1024
        ),
        cost_estimate=pl.CostEstimate(flops=10**10, bytes_accessed=10**7, transcendentals=0),
    )(hidden_act, out_grad, layer_stats, resident_stats, slot_block, layer_refresh)


def solution(mesh):
    in_specs = (
        P(("grp", "fsdp"), None),
        P(("grp", "fsdp"), None),
        P(("grp", "fsdp"), None),
        P(("grp", "fsdp"), None, None),
        P(),
        P(),
    )
    out_specs = (P(("grp", "fsdp"), None), P(("grp", "fsdp"), None), P(("grp", "fsdp"), None, None))
    return jax.shard_map(
        on_device, mesh=mesh, in_specs=in_specs, out_specs=out_specs, check_vma=False
    )
```

time: 581 us -> 75.5 us (0.13)
  waiting for transfers between devices: 492 us -> 0 us
  Pallas kernels: 0 us -> 67.8 us
  matrix products: 47.6 us -> 0 us
  between operations: 16.5 us -> 0.65 us
  other arithmetic: 11.6 us -> 0 us
    unnamed x3 -> x0, waiting for transfers between devices: 233 us -> none
    all_gather x1 -> x0, waiting for transfers between devices: 168 us -> none  [on_device(): section = lax.all_gather(grad_shard, 'fsdp', axis=0, tiled=True)]
    ppermute x1 -> x0, waiting for transfers between devices: 90.7 us -> none  [partner_2(): lax.ppermute(value, axis, [(i, i ^ 1 << stride) for i in range(lax.axis_s...]
    pallas_call x0 -> x1, Pallas kernels: none -> 67.8 us  [on_device(): pl.pallas_call(kernel, out_shape=(jax.ShapeDtypeStruct((4, 1024), F32), j...]
    dot_general x12 -> x0, matrix products: 47.6 us -> none  [the longest x3 13.1 us: fourth_root(): iterate = jnp.matmul(iterate, factor, precision=HIGHEST)]
  transfers between devices with their start and end apart: 3 -> 0, of which waited for: 3 -> 0; matrix products, arithmetic and copies ran while one was open for 10% -> 0% of each run, Pallas kernels for 0% -> 0%
where the time goes in v1:
time: 75.5 us; the launch traced here: 75.2 us
  Pallas kernels  67.8 us (90%)
  local copies, waits for them, and re-layouts  6.73 us (9%)
    pallas_call x1, Pallas kernels, on_device(): pl.pallas_call(kernel, out_shape=(jax.ShapeDtypeStruct((4, 1024), F32), j...  67.8 us
    unnamed x13, local copies, waits for them, and re-layouts  6.73 us

profile of v1, /device:TPU:1, one launch (start us, length us, event | category | flops | bytes accessed | tf_op | source)
XLA Modules:
  0.0 75.2 jit_solution(7071526740894211711)
XLA Ops:
  0.6 0.0 copy-start
  0.6 1.2 %copy-done = bf16[512,1024]{1,0:T(8,128)(2,1)S(1)} copy-done((bf16[512,1024]{1,0:T(8,128)(2,1)S(1)}, bf16[512,1024]{1,0:T(8,128)(2,1)}, u32[]{:S(2)}) %copy-start) | copy-done | bytes 1048600
  1.9 0.0 copy-start.1
  1.9 1.2 %copy-done.1 = bf16[512,1024]{1,0:T(8,128)(2,1)S(1)} copy-done((bf16[512,1024]{1,0:T(8,128)(2,1)S(1)}, bf16[512,1024]{1,0:T(8,128)(2,1)}, u32[]{:S(2)}) %copy-start.1) | copy-done | bytes 1048600
  3.1 0.0 copy-start.2
  3.1 0.8 %copy-done.2 = f32[16,512]{1,0:T(8,128)S(1)} copy-done((f32[16,512]{1,0:T(8,128)S(1)}, f32[16,512]{1,0:T(8,128)}, u32[]{:S(2)}) %copy-start.2) | copy-done | bytes 32792
  3.8 0.0 copy-start.3
  3.8 0.7 copy-done.3
  4.5 0.0 copy-start.4
  4.5 0.7 copy-done.4
  5.2 67.8 %shard_map.85 = (f32[4,1024]{1,0:T(4,128)S(1)}, f32[16,512]{1,0:T(8,128)S(1)}, f32[1,512,512]{2,1,0:T(8,128)S(1)}) custom-call(bf16[512,1024]{1,0:T(8,128)(2,1)S(1)} %copy-done, bf16[512,1024]{1,0:T(8,128)(2,1)S(1)} %copy-done.1, f32[16,512]{1,0:T(8,128)S(1)} %copy-done.2, f32[4,512,512]{2,1,0:T(8,128)} %res_any.1, s32[1024]{0:T(1024)S(1)} %copy-done.3, ...), custom_call_target="tpu_custom_call" | custom-call | flops 10000000000 | bytes 10000000 | tf_op jit(solution)/shard_map/pallas_call | solution.py:392
  73.0 0.6 copy.12
  73.6 0.6 copy.13
  74.2 1.0 %copy.14 = f32[1,512,512]{2,1,0:T(8,128)} copy(f32[1,512,512]{2,1,0:T(8,128)S(1)} %get-tuple-element.8) | data formatting | bytes 2097152
Async XLA Ops:
  0.6 1.2 %copy-start = (bf16[512,1024]{1,0:T(8,128)(2,1)S(1)}, bf16[512,1024]{1,0:T(8,128)(2,1)}, u32[]{:S(2)}) copy-start(bf16[512,1024]{1,0:T(8,128)(2,1)} %hid_any.1) | copy-start | bytes 3145732
  1.9 1.2 %copy-start.1 = (bf16[512,1024]{1,0:T(8,128)(2,1)S(1)}, bf16[512,1024]{1,0:T(8,128)(2,1)}, u32[]{:S(2)}) copy-start(bf16[512,1024]{1,0:T(8,128)(2,1)} %og_any.1) | copy-start | bytes 3145732
  3.1 0.8 %copy-start.2 = (f32[16,512]{1,0:T(8,128)S(1)}, f32[16,512]{1,0:T(8,128)}, u32[]{:S(2)}) copy-start(f32[16,512]{1,0:T(8,128)} %stats_in.1) | copy-start | bytes 98308
  3.8 0.7 copy-start.3
  4.5 0.7 copy-start.4

commit v2 on v1

v2 whole, which is shorter than its diff:
```python
import jax
import jax.numpy as jnp
from jax import lax
from jax.experimental import pallas as pl
from jax.experimental.pallas import tpu as pltpu
from jax.sharding import PartitionSpec as P

BPL = 16
EPSILON = 0.0001
MESH = pl.DeviceIdType.MESH
F32 = jnp.float32
BF16 = jnp.bfloat16
ZL, NY, NX, NZ = 4, 4, 4, 8
BLK = 512
HALF = 256
ROWS = 256
NCH = 2
PC = 4 // NCH
LAG = 2
HOOKS = (3, 3, 3, 3, 3)
SEMS = 100


def split(value):
    high = value.astype(BF16)
    return high, (value - high.astype(F32)).astype(BF16)


def dot(a, b, dims=(((1,), (0,)), ((), ()))):
    return lax.dot_general(a, b, dims, preferred_element_type=F32)


def kernel(
    hid_any, og_any, stats_any, res_any, slots_any, refresh_any,
    grad_out, stats_out, root_out,
    hid, og, stats_in, res, slot_block, refresh,
    g_send, g_own, core_recv, p1a, p1b, a1, b1, p2a, p2b, r, p3, fin, fin_other,
    tile, t_high, t_low, wide, pack, pack_recv,
    m0, m0_h, m0_l, q_h, q_l, r_h, r_l, w_h, w_l, p_f, p_h, p_l,
    in_sem, send_sem, recv_sem,
):
    grp = lax.axis_index("grp")
    f = lax.axis_index("fsdp")
    zl = f // 32
    y = (f // 8) % NY
    x = (f // 2) % NX
    c = f % 2
    z = grp * ZL + zl

    def dev(z_, y_, x_, c_):
        return (z_ // ZL, (z_ % ZL) * 32 + y_ * 8 + x_ * 2 + c_)

    partner = dev(z, y, x, 1 - c)
    xs = [dev(z, y, (x + k) % NX, c) for k in range(1, NX)]
    ys = [dev(z, (y + k) % NY, x, c) for k in range(1, NY)]
    zs = [dev((z + k) % NZ, y, x, c) for k in range(1, NZ)]

    sends = iter(range(SEMS))
    recvs = iter(range(SEMS))

    def copy(src, dst, to, recv=None):
        return pltpu.make_async_remote_copy(
            src_ref=src, dst_ref=dst, send_sem=send_sem.at[next(sends)],
            recv_sem=recv_sem.at[next(recvs)] if recv is None else recv,
            device_id=to, device_id_type=MESH,
        )

    barrier = pltpu.get_barrier_semaphore()
    peers = [partner] + xs + ys + zs
    cross = [dev(grp * ZL + (zl + k) % ZL, y, x, 1 - c) for k in range(1, ZL)]
    peers = peers + cross
    for peer in peers:
        pl.semaphore_signal(barrier, inc=1, device_id=peer, device_id_type=MESH)
    loads = [
        pltpu.make_async_copy(src, dst, in_sem.at[i])
        for i, (src, dst) in enumerate([
            (og_any, og), (hid_any, hid), (slots_any, slot_block), (refresh_any, refresh),
            (res_any, res), (stats_any, stats_in),
        ])
    ]
    for load in loads:
        load.start()

    def planes(i, j):
        return 4 * i + j * PC

    def grad_part(i, j, half):
        rows = pl.ds(planes(i, j) * 128, PC * 128)
        columns = pl.ds(pl.multiple_of(half * BLK, BLK), BLK)
        part = dot(hid[:, rows], og[:, columns], (((0,), (0,)), ((), ())))
        return part.reshape(PC, NY, NX, 8, BLK)

    chunks = [(i, j) for j in range(NCH) for i in range(2)]

    loads[0].wait()
    loads[1].wait()
    core = {}
    for n, (i, j) in enumerate(chunks):
        at = pl.ds(planes(i, j), PC)
        g_send[at] = grad_part(i, j, 1 - c)
        if n == 0:
            pl.semaphore_wait(barrier, len(peers))
        core[i, j] = copy(g_send.at[at], core_recv.at[at], partner)
        core[i, j].start()

    for load in loads[2:]:
        load.wait()
    own = (grp * 128 + f) * 4
    flags = [refresh[slot_block[own + l] // BPL] for l in range(4)]
    count = flags[0] + flags[1] + flags[2] + flags[3]
    pick0 = jnp.int32(0)
    pick1 = jnp.int32(0)
    before = jnp.int32(0)
    for l in range(4):
        pick0 = pick0 + jnp.where(before == 0, flags[l], 0) * l
        pick1 = pick1 + jnp.where(before == 1, flags[l], 0) * l
        before = before + flags[l]
    send_pick = jnp.where(grp == 0, pick1, pick0)
    own_pick = jnp.where(jnp.logical_and(grp == 1, count == 2), pick1, pick0)
    use_recv = count == 0

    row = lax.broadcasted_iota(jnp.int32, (HALF, HALF), 0)
    col = lax.broadcasted_iota(jnp.int32, (HALF, HALF), 1)
    lower_block = res[send_pick, HALF:, HALF:]
    pack[0:HALF] = res[send_pick, :HALF, HALF:]
    pack[HALF:2 * HALF] = jnp.where(row <= col, res[send_pick, :HALF, :HALF], lower_block)
    diagonal = jnp.sum(jnp.where(row == col, lower_block, 0.0), axis=0, keepdims=True)
    pack[2 * HALF:2 * HALF + 8] = jnp.broadcast_to(diagonal, (8, HALF))
    exchange = copy(pack, pack_recv, zs[3])
    exchange.start()

    def root_start():
        exchange.wait_recv()
        eye = (row == col).astype(F32)
        upper = pack_recv[HALF:2 * HALF]
        flipped = upper.T
        off = pack_recv[0:HALF]
        block_a = jnp.where(row <= col, upper, flipped)
        block_d = jnp.where(row > col, upper, flipped)
        block_d = jnp.where(row == col, jnp.broadcast_to(pack_recv[2 * HALF:2 * HALF + 1], (HALF, HALF)), block_d)
        total = jnp.zeros((1, 1), F32)
        for i, j, got in ((0, 0, block_a), (0, 1, off), (1, 0, off.T), (1, 1, block_d)):
            rows, cols = pl.ds(i * HALF, HALF), pl.ds(j * HALF, HALF)
            value = jnp.where(use_recv, got, res[own_pick, rows, cols])
            if i == j:
                value = value + EPSILON * eye
            m0[rows, cols] = value
            total = total + jnp.sum(value * value, axis=(0, 1), keepdims=True)
        zeta = 2.5 / jnp.sqrt(total + 1e-06)
        scale.append(jnp.sqrt(jnp.sqrt(zeta)))
        value = m0[...] * zeta
        m0[...] = value
        put(m0_h, m0_l, slice(None), value)

    scale = []

    def put(high, low, rows, value):
        value_h, value_l = split(value)
        high[rows, :] = value_h
        low[rows, :] = value_l

    def product(ah, al, bh, bl, rows):
        lead = ah[rows, :]
        return dot(lead, bh[...]) + dot(lead, bl[...]) + dot(al[rows, :], bh[...])

    def ident(i):
        r_ = lax.broadcasted_iota(jnp.int32, (ROWS, BLK), 0) + i * ROWS
        c_ = lax.broadcasted_iota(jnp.int32, (ROWS, BLK), 1)
        return (r_ == c_).astype(F32)

    def step1(i, rows):
        square = product(m0_h, m0_l, m0_h, m0_l, rows)
        m = m0[rows, :]
        put(w_h, w_l, rows, (5.0 * m - square) * 0.25)
        put(q_h, q_l, rows, (25.0 * ident(i) - 10.0 * m + square) * 0.0625)

    def step2(i, rows):
        put(r_h, r_l, rows, product(q_h, q_l, q_h, q_l, rows))

    def step3(i, rows):
        fifth = product(r_h, r_l, w_h, w_l, rows)
        factor = (5.0 * ident(i) - m0[rows, :]) * 0.25
        value = (5.0 * factor - fifth) * 0.25
        p_f[rows, :] = value
        put(p_h, p_l, rows, value)

    def step4(i, rows):
        put(q_h, q_l, rows, product(p_h, p_l, p_h, p_l, rows))

    def step5(i, rows):
        put(w_h, w_l, rows, product(p_h, p_l, m0_h, m0_l, rows))

    def step6(i, rows):
        fifth = product(r_h, r_l, w_h, w_l, rows)
        root_out[0, rows, :] = (5.0 * p_f[rows, :] - fifth) * (0.25 * scale[0])

    def root_steps():
        yield root_start()
        for body in (step1, step2, step3, step4, step5, step2, step6):
            for i in range(BLK // ROWS):
                yield body(i, pl.ds(i * ROWS, ROWS))

    steps = root_steps()

    def run(number):
        for _ in range(number):
            next(steps, None)

    phase1, phase2, phase3 = {}, {}, []
    for i, j in chunks:
        at = pl.ds(planes(i, j), PC)
        part = grad_part(i, j, c)
        core[i, j].wait_recv()
        g_own[at] = part + core_recv[at]
        here = pl.ds(j * PC, PC)
        group = []
        for k in range(1, 4):
            if i == 0:
                item = copy(g_own.at[at, :, (x + k) % NX], p1a.at[k - 1, here], xs[k - 1])
            else:
                item = copy(g_own.at[at, (y + k) % NY], p1b.at[k - 1, here], ys[k - 1])
            item.start()
            group.append(item)
        phase1[i, j] = group

    def second(i, j):
        here = pl.ds(j * PC, PC)
        at = pl.ds(planes(i, j), PC)
        for item in phase1[i, j]:
            item.wait_recv()
        got, total = (p1a, a1) if i == 0 else (p1b, b1)
        mine = g_own[at, :, x] if i == 0 else g_own[at, y]
        total[here] = mine + got[0, here] + got[1, here] + got[2, here]
        group = []
        for k in range(1, 4):
            if i == 0:
                item = copy(total.at[here, (y + k) % NY], p2a.at[k - 1, here], ys[k - 1])
            else:
                item = copy(total.at[here, (x + k) % NX], p2b.at[k - 1, here], xs[k - 1])
            item.start()
            group.append(item)
        phase2[i, j] = group

    z_base = [next(recvs) for _ in range(NZ)][0]

    def third(i, j):
        here = pl.ds(j * PC, PC)
        for item in phase2[i, j]:
            item.wait_recv()
        got, total, at = (p2a, a1, y) if i == 0 else (p2b, b1, x)
        r[pl.ds(planes(i, j), PC)] = total[here, at] + got[0, here] + got[1, here] + got[2, here]
        for q in range(PC):
            p = planes(i, j) + q
            item = copy(r.at[p], p3.at[z], dev(jnp.int32(p), y, x, c), recv_sem.at[z_base + z])
            pl.when(z != p)(item.start)
            phase3.append((z != p, item))

    for n, (i, j) in enumerate(chunks):
        second(i, j)
        if n >= LAG:
            third(*chunks[n - LAG])
    for n in range(len(chunks) - LAG, len(chunks)):
        third(*chunks[n])

    run(HOOKS[0])
    mine = r[z]
    for k in range(1, NZ):
        source = (z + k) % NZ
        pltpu.make_async_remote_copy(
            src_ref=r.at[z], dst_ref=p3.at[source], send_sem=send_sem.at[0],
            recv_sem=recv_sem.at[z_base + source], device_id=partner, device_id_type=MESH,
        ).wait_recv()
        mine = mine + p3[source]
    fin[...] = mine

    gz_base = [next(recvs) for _ in range(2)][0]
    near = c == zl // 2
    gz = []
    for t in range(2):
        to = 2 * c + t
        item = copy(
            fin, tile.at[zl, y, x], dev(grp * ZL + to, y, x, zl // 2), recv_sem.at[gz_base + zl % 2]
        )
        sent = jnp.logical_not(jnp.logical_and(near, to == zl))
        pl.when(sent)(item.start)
        gz.append((sent, item))
    swap = copy(fin, fin_other, partner)
    swap.start()

    run(HOOKS[1])

    def keep():
        tile[zl, y, x] = mine

    pl.when(near)(keep)
    for t in range(2):
        source = 2 * c + t
        item = pltpu.make_async_remote_copy(
            src_ref=fin, dst_ref=tile.at[source, y, x], send_sem=send_sem.at[0],
            recv_sem=recv_sem.at[gz_base + t], device_id=partner, device_id_type=MESH,
        )
        pl.when(jnp.logical_not(jnp.logical_and(near, source == zl)))(item.wait_recv)

    first, later, forward = [], [], []
    for side in range(2):
        two = pl.ds(2 * side, 2)
        one_peers, two_peers = (ys, xs) if side == 0 else (xs, ys)
        slabs = [
            tile.at[two, :, (x + 4 - k) % NX] if side == 0 else tile.at[two, (y + 4 - k) % NY]
            for k in range(4)
        ]
        spot = tile.at[two, y, x]
        if side == 0:
            ids = [(next(sends), next(recvs)) for _ in range(10)]

        def make(src, to, n):
            return pltpu.make_async_remote_copy(
                src_ref=src, dst_ref=src, send_sem=send_sem.at[ids[n][0]], recv_sem=recv_sem.at[ids[n][1]],
                device_id=to, device_id_type=MESH,
            )

        first.append([make(spot, one_peers[k], k) for k in range(3)])
        later.append([make(slabs[0], two_peers[k], 3 + k) for k in range(3)])
        forward.append([make(slabs[k], partner, 6 + k) for k in range(4)])

    def both(body):
        pl.when(c == 0)(lambda: body(0))
        pl.when(c == 1)(lambda: body(1))

    def gather_first(side):
        for item in first[side]:
            item.start()

    def gather_later(side):
        for item in first[side]:
            item.wait_recv()
        for item in later[side]:
            item.start()
        forward[side][0].start()

    def gather_end(side):
        for k in range(1, 4):
            later[side][k - 1].wait_recv()
            forward[side][k].start()

    def gather_take(side):
        for k in range(4):
            forward[1 - side][k].wait_recv()

    both(gather_first)
    run(HOOKS[2])
    both(gather_later)
    run(HOOKS[3])
    both(gather_end)
    run(HOOKS[4])

    swap.wait_recv()
    low = jnp.where(c == 0, fin[...], fin_other[...])
    high = jnp.where(c == 0, fin_other[...], fin[...])
    grad_out[:, :BLK] = jnp.where(c == 0, low[:4], low[4:])
    grad_out[:, BLK:] = jnp.where(c == 0, high[:4], high[4:])
    both(gather_take)

    t_value = tile[...].reshape(BLK, BLK)
    t_h, t_l = split(t_value)
    t_high[...] = t_h
    t_low[...] = t_l
    at = (f % 32) * 16

    def left():
        dims = (((1,), (1,)), ((), ()))
        rows = pl.ds(pl.multiple_of(at, 16), 16)
        lead_h, lead_l = t_high[rows, :], t_low[rows, :]
        part = dot(lead_h, t_high[...], dims) + dot(lead_h, t_low[...], dims) + dot(lead_l, t_high[...], dims)
        stats_out[...] = stats_in[...] + part * (1.0 / BLK)

    def right():
        dims = (((0,), (0,)), ((), ()))
        columns = pl.ds(pl.multiple_of(at // 128 * 128, 128), 128)
        lead_h, lead_l = t_high[:, columns], t_low[:, columns]
        wide[...] = dot(lead_h, t_high[...], dims) + dot(lead_h, t_low[...], dims) + dot(lead_l, t_high[...], dims)
        part = wide[pl.ds(pl.multiple_of(at % 128, 16), 16), :]
        stats_out[...] = stats_in[...] + part * (1.0 / BLK)

    pl.when(zl % 2 == 0)(left)
    pl.when(zl % 2 == 1)(right)
    run(20)

    for group in [list(core.values()), [exchange, swap]] + list(phase1.values()) + list(phase2.values()):
        for item in group:
            item.wait_send()
    for sent, item in phase3 + gz:
        pl.when(sent)(item.wait_send)

    def sent_all(side):
        for item in first[side] + later[side] + forward[side]:
            item.wait_send()

    both(sent_all)


def on_device(hidden_act, out_grad, layer_stats, resident_stats, slot_block, layer_refresh):
    vmem = pl.BlockSpec(memory_space=pltpu.VMEM)
    hbm = pl.BlockSpec(memory_space=pltpu.HBM)
    square = (BLK, BLK)
    piece = (8, BLK)
    scratch = [
        pltpu.VMEM(hidden_act.shape, BF16),
        pltpu.VMEM(out_grad.shape, BF16),
        pltpu.VMEM(layer_stats.shape, F32),
        pltpu.VMEM(resident_stats.shape, F32),
        pltpu.SMEM(slot_block.shape, jnp.int32),
        pltpu.SMEM(layer_refresh.shape, jnp.int32),
        pltpu.VMEM((NZ, NY, NX) + piece, F32),
        pltpu.VMEM((NZ, NY, NX) + piece, F32),
        pltpu.VMEM((NZ, NY, NX) + piece, F32),
        pltpu.VMEM((3, 4, NY) + piece, F32),
        pltpu.VMEM((3, 4, NX) + piece, F32),
        pltpu.VMEM((4, NY) + piece, F32),
        pltpu.VMEM((4, NX) + piece, F32),
        pltpu.VMEM((3, 4) + piece, F32),
        pltpu.VMEM((3, 4) + piece, F32),
        pltpu.VMEM((NZ,) + piece, F32),
        pltpu.VMEM((NZ,) + piece, F32),
        pltpu.VMEM(piece, F32),
        pltpu.VMEM(piece, F32),
        pltpu.VMEM((ZL, NY, NX) + piece, F32),
        pltpu.VMEM(square, BF16),
        pltpu.VMEM(square, BF16),
        pltpu.VMEM((128, BLK), F32),
        pltpu.VMEM((2 * HALF + 8, HALF), F32),
        pltpu.VMEM((2 * HALF + 8, HALF), F32),
        pltpu.VMEM(square, F32),
        pltpu.VMEM(square, BF16),
        pltpu.VMEM(square, BF16),
        pltpu.VMEM(square, BF16),
        pltpu.VMEM(square, BF16),
        pltpu.VMEM(square, BF16),
        pltpu.VMEM(square, BF16),
        pltpu.VMEM(square, BF16),
        pltpu.VMEM(square, BF16),
        pltpu.VMEM(square, F32),
        pltpu.VMEM(square, BF16),
        pltpu.VMEM(square, BF16),
        pltpu.SemaphoreType.DMA((6,)),
        pltpu.SemaphoreType.DMA((SEMS,)),
        pltpu.SemaphoreType.DMA((SEMS,)),
    ]
    return pl.pallas_call(
        kernel,
        out_shape=(
            jax.ShapeDtypeStruct((4, 1024), F32),
            jax.ShapeDtypeStruct(layer_stats.shape, F32),
            jax.ShapeDtypeStruct((1, BLK, BLK), F32),
        ),
        in_specs=[hbm] * 6,
        out_specs=(vmem, vmem, vmem),
        scratch_shapes=scratch,
        compiler_params=pltpu.CompilerParams(
            collective_id=0, has_side_effects=True, vmem_limit_bytes=48 * 1024 * 1024
        ),
        cost_estimate=pl.CostEstimate(flops=10**10, bytes_accessed=10**7, transcendentals=0),
    )(hidden_act, out_grad, layer_stats, resident_stats, slot_block, layer_refresh)


def solution(mesh):
    in_specs = (
        P(("grp", "fsdp"), None),
        P(("grp", "fsdp"), None),
        P(("grp", "fsdp"), None),
        P(("grp", "fsdp"), None, None),
        P(),
        P(),
    )
    out_specs = (P(("grp", "fsdp"), None), P(("grp", "fsdp"), None), P(("grp", "fsdp"), None, None))
    return jax.shard_map(
        on_device, mesh=mesh, in_specs=in_specs, out_specs=out_specs, check_vma=False
    )
```

time: 75.5 us -> 64.2 us (0.85)
  Pallas kernels: 67.8 us -> 56.5 us
    pallas_call x1, Pallas kernels: 67.8 us -> 56.5 us  [on_device(): pl.pallas_call(kernel, out_shape=(jax.ShapeDtypeStruct((4, 1024), F32), j...]
where the time goes in v2:
time: 64.2 us; the launch traced here: 63.9 us
  Pallas kernels  56.5 us (88%)
  local copies, waits for them, and re-layouts  6.73 us (10%)
  between operations  0.65 us (1%)
    pallas_call x1, Pallas kernels, on_device(): pl.pallas_call(kernel, out_shape=(jax.ShapeDtypeStruct((4, 1024), F32), j...  56.5 us
    unnamed x13, local copies, waits for them, and re-layouts  6.73 us

profile of v2, /device:TPU:1, one launch (start us, length us, event | category | flops | bytes accessed | tf_op | source)
XLA Modules:
  0.0 63.9 jit_solution(701614345148950614)
XLA Ops:
  0.6 0.0 copy-start
  0.6 1.2 %copy-done = bf16[512,1024]{1,0:T(8,128)(2,1)S(1)} copy-done((bf16[512,1024]{1,0:T(8,128)(2,1)S(1)}, bf16[512,1024]{1,0:T(8,128)(2,1)}, u32[]{:S(2)}) %copy-start) | copy-done | bytes 1048600
  1.9 0.0 copy-start.1
  1.9 1.2 %copy-done.1 = bf16[512,1024]{1,0:T(8,128)(2,1)S(1)} copy-done((bf16[512,1024]{1,0:T(8,128)(2,1)S(1)}, bf16[512,1024]{1,0:T(8,128)(2,1)}, u32[]{:S(2)}) %copy-start.1) | copy-done | bytes 1048600
  3.1 0.0 copy-start.2
  3.1 0.8 %copy-done.2 = f32[16,512]{1,0:T(8,128)S(1)} copy-done((f32[16,512]{1,0:T(8,128)S(1)}, f32[16,512]{1,0:T(8,128)}, u32[]{:S(2)}) %copy-start.2) | copy-done | bytes 32792
  3.8 0.0 copy-start.3
  3.8 0.7 %copy-done.3 = s32[1024]{0:T(1024)S(1)} copy-done((s32[1024]{0:T(1024)S(1)}, s32[1024]{0:T(1024)}, u32[]{:S(2)}) %copy-start.3) | copy-done | bytes 4120
  4.5 0.0 copy-start.4
  4.5 0.7 %copy-done.4 = s32[64]{0:T(128)S(1)} copy-done((s32[64]{0:T(128)S(1)}, s32[64]{0:T(128)}, u32[]{:S(2)}) %copy-start.4) | copy-done | bytes 280
  5.2 56.5 %shard_map.85 = (f32[4,1024]{1,0:T(4,128)S(1)}, f32[16,512]{1,0:T(8,128)S(1)}, f32[1,512,512]{2,1,0:T(8,128)S(1)}) custom-call(bf16[512,1024]{1,0:T(8,128)(2,1)S(1)} %copy-done, bf16[512,1024]{1,0:T(8,128)(2,1)S(1)} %copy-done.1, f32[16,512]{1,0:T(8,128)S(1)} %copy-done.2, f32[4,512,512]{2,1,0:T(8,128)} %res_any.1, s32[1024]{0:T(1024)S(1)} %copy-done.3, ...), custom_call_target="tpu_custom_call" | custom-call | flops 10000000000 | bytes 10000000 | tf_op jit(solution)/shard_map/pallas_call | solution.py:449
  61.7 0.6 copy.12
  62.3 0.6 copy.13
  62.9 1.0 %copy.14 = f32[1,512,512]{2,1,0:T(8,128)} copy(f32[1,512,512]{2,1,0:T(8,128)S(1)} %get-tuple-element.8) | data formatting | bytes 2097152
Async XLA Ops:
  0.6 1.2 %copy-start = (bf16[512,1024]{1,0:T(8,128)(2,1)S(1)}, bf16[512,1024]{1,0:T(8,128)(2,1)}, u32[]{:S(2)}) copy-start(bf16[512,1024]{1,0:T(8,128)(2,1)} %hid_any.1) | copy-start | bytes 3145732
  1.9 1.2 %copy-start.1 = (bf16[512,1024]{1,0:T(8,128)(2,1)S(1)}, bf16[512,1024]{1,0:T(8,128)(2,1)}, u32[]{:S(2)}) copy-start(bf16[512,1024]{1,0:T(8,128)(2,1)} %og_any.1) | copy-start | bytes 3145732
  3.1 0.8 %copy-start.2 = (f32[16,512]{1,0:T(8,128)S(1)}, f32[16,512]{1,0:T(8,128)}, u32[]{:S(2)}) copy-start(f32[16,512]{1,0:T(8,128)} %stats_any.1) | copy-start | bytes 98308
  3.8 0.7 %copy-start.3 = (s32[1024]{0:T(1024)S(1)}, s32[1024]{0:T(1024)}, u32[]{:S(2)}) copy-start(s32[1024]{0:T(1024)} %slots_any.1) | copy-start | bytes 12292
  4.5 0.7 %copy-start.4 = (s32[64]{0:T(128)S(1)}, s32[64]{0:T(128)}, u32[]{:S(2)}) copy-start(s32[64]{0:T(128)} %refresh_any.1) | copy-start | bytes 772

commit v3 on v2

--- a/solution.py
+++ b/solution.py
@@ -17,7 +17,7 @@
 NCH = 2
 PC = 4 // NCH
 LAG = 2
-HOOKS = (3, 3, 3, 3, 3)
+HOOKS = (0, 8, 7, 0)
 SEMS = 100
 
 
@@ -34,7 +34,7 @@
     hid_any, og_any, stats_any, res_any, slots_any, refresh_any,
     grad_out, stats_out, root_out,
     hid, og, stats_in, res, slot_block, refresh,
-    g_send, g_own, core_recv, p1a, p1b, a1, b1, p2a, p2b, r, p3, fin, fin_other,
+    g_send, g_own, core_recv, s1a, s1b, p1a, p1b, a1, b1, p2a, p2b, r, p3, fin, fin_other,
     tile, t_high, t_low, wide, pack, pack_recv,
     m0, m0_h, m0_l, q_h, q_l, r_h, r_l, w_h, w_l, p_f, p_h, p_l,
     in_sem, send_sem, recv_sem,
@@ -65,16 +65,32 @@
             device_id=to, device_id_type=MESH,
         )
 
+    keeper = zl // 2
+
+    def gather_to(t, k):
+        to_y = jnp.where(keeper == 0, (y + k) % NY, y)
+        to_x = jnp.where(keeper == 0, x, (x + k) % NX)
+        return dev(grp * ZL + 2 * c + t, to_y, to_x, keeper)
+
+    def gather_from(t, k):
+        from_y = jnp.where(c == 0, (y + 4 - k) % NY, y)
+        from_x = jnp.where(c == 0, x, (x + 4 - k) % NX)
+        return dev(grp * ZL + 2 * c + t, from_y, from_x, keeper)
+
     barrier = pltpu.get_barrier_semaphore()
     peers = [partner] + xs + ys + zs
     cross = [dev(grp * ZL + (zl + k) % ZL, y, x, 1 - c) for k in range(1, ZL)]
     peers = peers + cross
+    for t in range(2):
+        for k in range(1, 4):
+            peers.append(gather_to(t, k))
+            peers.append(gather_from(t, k))
     for peer in peers:
         pl.semaphore_signal(barrier, inc=1, device_id=peer, device_id_type=MESH)
     loads = [
         pltpu.make_async_copy(src, dst, in_sem.at[i])
         for i, (src, dst) in enumerate([
-            (og_any, og), (hid_any, hid), (slots_any, slot_block), (refresh_any, refresh),
+            (slots_any, slot_block), (refresh_any, refresh), (og_any, og), (hid_any, hid),
             (res_any, res), (stats_any, stats_in),
         ])
     ]
@@ -94,17 +110,6 @@
 
     loads[0].wait()
     loads[1].wait()
-    core = {}
-    for n, (i, j) in enumerate(chunks):
-        at = pl.ds(planes(i, j), PC)
-        g_send[at] = grad_part(i, j, 1 - c)
-        if n == 0:
-            pl.semaphore_wait(barrier, len(peers))
-        core[i, j] = copy(g_send.at[at], core_recv.at[at], partner)
-        core[i, j].start()
-
-    for load in loads[2:]:
-        load.wait()
     own = (grp * 128 + f) * 4
     flags = [refresh[slot_block[own + l] // BPL] for l in range(4)]
     count = flags[0] + flags[1] + flags[2] + flags[3]
@@ -119,15 +124,30 @@
     own_pick = jnp.where(jnp.logical_and(grp == 1, count == 2), pick1, pick0)
     use_recv = count == 0
 
+    loads[2].wait()
+    loads[3].wait()
+    core = {}
+    for i, j in chunks:
+        at = pl.ds(planes(i, j), PC)
+        g_send[at] = grad_part(i, j, 1 - c)
+        core[i, j] = copy(g_send.at[at], core_recv.at[at], partner)
+
     row = lax.broadcasted_iota(jnp.int32, (HALF, HALF), 0)
     col = lax.broadcasted_iota(jnp.int32, (HALF, HALF), 1)
+    loads[4].wait()
+    loads[5].wait()
     lower_block = res[send_pick, HALF:, HALF:]
     pack[0:HALF] = res[send_pick, :HALF, HALF:]
     pack[HALF:2 * HALF] = jnp.where(row <= col, res[send_pick, :HALF, :HALF], lower_block)
     diagonal = jnp.sum(jnp.where(row == col, lower_block, 0.0), axis=0, keepdims=True)
     pack[2 * HALF:2 * HALF + 8] = jnp.broadcast_to(diagonal, (8, HALF))
     exchange = copy(pack, pack_recv, zs[3])
+
+    pl.semaphore_wait(barrier, len(peers))
+    core[0, 0].start()
     exchange.start()
+    for item in chunks[1:]:
+        core[item].start()
 
     def root_start():
         exchange.wait_recv()
@@ -206,31 +226,51 @@
         for _ in range(number):
             next(steps, None)
 
-    phase1, phase2, phase3 = {}, {}, []
+    met, phase1, phase2, phase3 = {}, {}, {}, []
+    half_recv, whole_recv = (s1a, s1b), (p1a, p1b)
+
+    def axis(i):
+        return (xs[0], xs[2]) if i == 0 else (ys[0], ys[2])
+
+    def spot(i, plane, k):
+        return g_own.at[plane, :, (x + k) % NX] if i == 0 else g_own.at[plane, (y + k) % NY]
+
     for i, j in chunks:
         at = pl.ds(planes(i, j), PC)
         part = grad_part(i, j, c)
         core[i, j].wait_recv()
         g_own[at] = part + core_recv[at]
-        here = pl.ds(j * PC, PC)
-        group = []
-        for k in range(1, 4):
-            if i == 0:
-                item = copy(g_own.at[at, :, (x + k) % NX], p1a.at[k - 1, here], xs[k - 1])
-            else:
-                item = copy(g_own.at[at, (y + k) % NY], p1b.at[k - 1, here], ys[k - 1])
+        low, high = planes(i, j), planes(i, j) + 1
+        plus, minus = axis(i)
+        met[i, j] = [
+            copy(spot(i, low, 2), half_recv[i].at[0, j], plus),
+            copy(spot(i, high, 2), half_recv[i].at[1, j], minus),
+        ]
+        phase1[i, j] = [
+            copy(spot(i, high, 1), whole_recv[i].at[0, 2 * j + 1], plus),
+            copy(spot(i, low, 3), whole_recv[i].at[1, 2 * j], minus),
+        ]
+        for item in met[i, j] + phase1[i, j]:
             item.start()
-            group.append(item)
-        phase1[i, j] = group
+    for i, j in chunks:
+        low, high = planes(i, j), planes(i, j) + 1
+        plus, minus = axis(i)
+        for side, (plane, k, to) in enumerate(((low, 1, plus), (high, 3, minus))):
+            met[i, j][side].wait_recv()
+            there = spot(i, plane, k)
+            there[...] = there[...] + half_recv[i][side, j]
+            item = copy(there, whole_recv[i].at[side, 2 * j + side], to)
+            item.start()
+            phase1[i, j].append(item)
 
     def second(i, j):
         here = pl.ds(j * PC, PC)
         at = pl.ds(planes(i, j), PC)
         for item in phase1[i, j]:
             item.wait_recv()
-        got, total = (p1a, a1) if i == 0 else (p1b, b1)
+        got, total = whole_recv[i], (a1, b1)[i]
         mine = g_own[at, :, x] if i == 0 else g_own[at, y]
-        total[here] = mine + got[0, here] + got[1, here] + got[2, here]
+        total[here] = mine + got[0, here] + got[1, here]
         group = []
         for k in range(1, 4):
             if i == 0:
@@ -273,45 +313,51 @@
         mine = mine + p3[source]
     fin[...] = mine
 
-    gz_base = [next(recvs) for _ in range(2)][0]
-    near = c == zl // 2
+    gz_base = [next(recvs) for _ in range(8)][0]
+    near = c == keeper
     gz = []
-    for t in range(2):
-        to = 2 * c + t
-        item = copy(
-            fin, tile.at[zl, y, x], dev(grp * ZL + to, y, x, zl // 2), recv_sem.at[gz_base + zl % 2]
-        )
-        sent = jnp.logical_not(jnp.logical_and(near, to == zl))
-        pl.when(sent)(item.start)
-        gz.append((sent, item))
+    for k in range(4):
+        for t in range(2):
+            item = copy(
+                fin, tile.at[zl, y, x], gather_to(t, k), recv_sem.at[gz_base + 4 * (zl % 2) + k]
+            )
+            if k == 0:
+                sent = jnp.logical_not(jnp.logical_and(near, 2 * c + t == zl))
+                pl.when(sent)(item.start)
+                gz.append((sent, item))
+            else:
+                item.start()
+                gz.append((None, item))
     swap = copy(fin, fin_other, partner)
     swap.start()
 
-    run(HOOKS[1])
-
     def keep():
         tile[zl, y, x] = mine
 
     pl.when(near)(keep)
-    for t in range(2):
-        source = 2 * c + t
-        item = pltpu.make_async_remote_copy(
-            src_ref=fin, dst_ref=tile.at[source, y, x], send_sem=send_sem.at[0],
-            recv_sem=recv_sem.at[gz_base + t], device_id=partner, device_id_type=MESH,
-        )
-        pl.when(jnp.logical_not(jnp.logical_and(near, source == zl)))(item.wait_recv)
-
-    first, later, forward = [], [], []
+    run(HOOKS[1])
+    for k in range(4):
+        for t in range(2):
+            source = 2 * c + t
+            from_y = jnp.where(c == 0, (y + 4 - k) % NY, y)
+            from_x = jnp.where(c == 0, x, (x + 4 - k) % NX)
+            item = pltpu.make_async_remote_copy(
+                src_ref=fin, dst_ref=tile.at[source, from_y, from_x], send_sem=send_sem.at[0],
+                recv_sem=recv_sem.at[gz_base + 4 * t + k], device_id=partner, device_id_type=MESH,
+            )
+            if k == 0:
+                pl.when(jnp.logical_not(jnp.logical_and(near, source == zl)))(item.wait_recv)
+            else:
+                item.wait_recv()
+
+    ids = [(next(sends), next(recvs)) for _ in range(7)]
+    later, forward = [], []
     for side in range(2):
         two = pl.ds(2 * side, 2)
-        one_peers, two_peers = (ys, xs) if side == 0 else (xs, ys)
         slabs = [
             tile.at[two, :, (x + 4 - k) % NX] if side == 0 else tile.at[two, (y + 4 - k) % NY]
             for k in range(4)
         ]
-        spot = tile.at[two, y, x]
-        if side == 0:
-            ids = [(next(sends), next(recvs)) for _ in range(10)]
 
         def make(src, to, n):
             return pltpu.make_async_remote_copy(
@@ -319,40 +365,31 @@
                 device_id=to, device_id_type=MESH,
             )
 
-        first.append([make(spot, one_peers[k], k) for k in range(3)])
-        later.append([make(slabs[0], two_peers[k], 3 + k) for k in range(3)])
-        forward.append([make(slabs[k], partner, 6 + k) for k in range(4)])
+        later.append([make(slabs[0], (xs, ys)[side][k], k) for k in range(3)])
+        forward.append([make(slabs[k], partner, 3 + k) for k in range(4)])
 
     def both(body):
         pl.when(c == 0)(lambda: body(0))
         pl.when(c == 1)(lambda: body(1))
 
-    def gather_first(side):
-        for item in first[side]:
-            item.start()
-
     def gather_later(side):
-        for item in first[side]:
-            item.wait_recv()
         for item in later[side]:
             item.start()
         forward[side][0].start()
 
     def gather_end(side):
-        for k in range(1, 4):
+        for k in (1, 3, 2):
             later[side][k - 1].wait_recv()
             forward[side][k].start()
 
     def gather_take(side):
-        for k in range(4):
+        for k in (0, 1, 3, 2):
             forward[1 - side][k].wait_recv()
 
-    both(gather_first)
+    both(gather_later)
     run(HOOKS[2])
-    both(gather_later)
+    both(gather_end)
     run(HOOKS[3])
-    both(gather_end)
-    run(HOOKS[4])
 
     swap.wait_recv()
     low = jnp.where(c == 0, fin[...], fin_other[...])
@@ -386,14 +423,17 @@
     pl.when(zl % 2 == 1)(right)
     run(20)
 
-    for group in [list(core.values()), [exchange, swap]] + list(phase1.values()) + list(phase2.values()):
+    for group in [list(core.values()), [exchange, swap]] + list(met.values()) + list(phase1.values()) + list(phase2.values()):
         for item in group:
             item.wait_send()
     for sent, item in phase3 + gz:
-        pl.when(sent)(item.wait_send)
+        if sent is None:
+            item.wait_send()
+        else:
+            pl.when(sent)(item.wait_send)
 
     def sent_all(side):
-        for item in first[side] + later[side] + forward[side]:
+        for item in later[side] + forward[side]:
             item.wait_send()
 
     both(sent_all)
@@ -414,8 +454,10 @@
         pltpu.VMEM((NZ, NY, NX) + piece, F32),
         pltpu.VMEM((NZ, NY, NX) + piece, F32),
         pltpu.VMEM((NZ, NY, NX) + piece, F32),
-        pltpu.VMEM((3, 4, NY) + piece, F32),
-        pltpu.VMEM((3, 4, NX) + piece, F32),
+        pltpu.VMEM((2, 2, NY) + piece, F32),
+        pltpu.VMEM((2, 2, NX) + piece, F32),
+        pltpu.VMEM((2, 4, NY) + piece, F32),
+        pltpu.VMEM((2, 4, NX) + piece, F32),
         pltpu.VMEM((4, NY) + piece, F32),
         pltpu.VMEM((4, NX) + piece, F32),
         pltpu.VMEM((3, 4) + piece, F32),
@@ -460,7 +502,10 @@
             collective_id=0, has_side_effects=True, vmem_limit_bytes=48 * 1024 * 1024
         ),
         cost_estimate=pl.CostEstimate(flops=10**10, bytes_accessed=10**7, transcendentals=0),
-    )(hidden_act, out_grad, layer_stats, resident_stats, slot_block, layer_refresh)
+    )(*[
+        pltpu.with_memory_space_constraint(value, pltpu.HBM)
+        for value in (hidden_act, out_grad, layer_stats, resident_stats, slot_block, layer_refresh)
+    ])
 
 
 def solution(mesh):

time: 64.2 us -> 58 us (0.903)
  local copies, waits for them, and re-layouts: 6.73 us -> 2.19 us
  Pallas kernels: 56.5 us -> 55.1 us
    unnamed x13 -> x3, local copies, waits for them, and re-layouts: 6.73 us -> 2.19 us
    pallas_call x1, Pallas kernels: 56.5 us -> 55.1 us  [on_device(): pl.pallas_call(kernel, out_shape=(jax.ShapeDtypeStruct((4, 1024), F32), j...]
where the time goes in v3:
time: 58 us; the launch traced here: 57.9 us
  Pallas kernels  55.1 us (95%)
  local copies, waits for them, and re-layouts  2.19 us (4%)
  between operations  0.64 us (1%)
    pallas_call x1, Pallas kernels, on_device(): pl.pallas_call(kernel, out_shape=(jax.ShapeDtypeStruct((4, 1024), F32), j...  55.1 us
    unnamed x3, local copies, waits for them, and re-layouts  2.19 us

profile of v3, /device:TPU:1, one launch (start us, length us, event | category | flops | bytes accessed | tf_op | source)
XLA Modules:
  0.0 57.9 jit_solution(3515817288291437347)
XLA Ops:
  0.6 55.1 %shard_map.85 = (f32[4,1024]{1,0:T(4,128)S(1)}, f32[16,512]{1,0:T(8,128)S(1)}, f32[1,512,512]{2,1,0:T(8,128)S(1)}) custom-call(bf16[512,1024]{1,0:T(8,128)(2,1)} %hid_any.1, bf16[512,1024]{1,0:T(8,128)(2,1)} %og_any.1, f32[16,512]{1,0:T(8,128)} %stats_any.1, f32[4,512,512]{2,1,0:T(8,128)} %res_any.1, s32[1024]{0:T(1024)} %slots_any.1, s32[64]{0:T(128)} %refresh_any.1), custom_call_target="tpu_custom_call" | custom-call | flops 10000000000 | bytes 10000000 | tf_op jit(solution)/shard_map/pallas_call | solution.py:491
  55.7 0.6 %copy.12 = f32[4,1024]{1,0:T(4,128)} copy(f32[4,1024]{1,0:T(4,128)S(1)} %get-tuple-element.6) | data formatting | bytes 32768
  56.3 0.6 %copy.13 = f32[16,512]{1,0:T(8,128)} copy(f32[16,512]{1,0:T(8,128)S(1)} %get-tuple-element.7) | data formatting | bytes 65536
  56.9 1.0 %copy.14 = f32[1,512,512]{2,1,0:T(8,128)} copy(f32[1,512,512]{2,1,0:T(8,128)S(1)} %get-tuple-element.8) | data formatting | bytes 2097152

commit v4 on v3

--- a/solution.py
+++ b/solution.py
@@ -19,6 +19,7 @@
 LAG = 2
 HOOKS = (0, 8, 7, 0)
 SEMS = 100
+CUTS = (400, 408)
 
 
 def split(value):
@@ -141,16 +142,20 @@
     pack[HALF:2 * HALF] = jnp.where(row <= col, res[send_pick, :HALF, :HALF], lower_block)
     diagonal = jnp.sum(jnp.where(row == col, lower_block, 0.0), axis=0, keepdims=True)
     pack[2 * HALF:2 * HALF + 8] = jnp.broadcast_to(diagonal, (8, HALF))
-    exchange = copy(pack, pack_recv, zs[3])
+    exchange = []
+    for first, last in zip((0,) + CUTS, CUTS + (2 * HALF + 8,)):
+        rows = pl.ds(first, last - first)
+        exchange.append(copy(pack.at[rows], pack_recv.at[rows], zs[3]))
 
     pl.semaphore_wait(barrier, len(peers))
     core[0, 0].start()
-    exchange.start()
+    exchange[0].start()
     for item in chunks[1:]:
         core[item].start()
 
     def root_start():
-        exchange.wait_recv()
+        for item in exchange:
+            item.wait_recv()
         eye = (row == col).astype(F32)
         upper = pack_recv[HALF:2 * HALF]
         flipped = upper.T
@@ -297,11 +302,14 @@
 
     for n, (i, j) in enumerate(chunks):
         second(i, j)
+        if n == 1:
+            exchange[1].start()
         if n >= LAG:
             third(*chunks[n - LAG])
     for n in range(len(chunks) - LAG, len(chunks)):
         third(*chunks[n])
 
+    exchange[2].start()
     run(HOOKS[0])
     mine = r[z]
     for k in range(1, NZ):
@@ -423,7 +431,7 @@
     pl.when(zl % 2 == 1)(right)
     run(20)
 
-    for group in [list(core.values()), [exchange, swap]] + list(met.values()) + list(phase1.values()) + list(phase2.values()):
+    for group in [list(core.values()), exchange, [swap]] + list(met.values()) + list(phase1.values()) + list(phase2.values()):
         for item in group:
             item.wait_send()
     for sent, item in phase3 + gz:
@@ -437,6 +445,17 @@
             item.wait_send()
 
     both(sent_all)
+
+
+def deliver(grad_any, stats_any, root_any, grad_to, stats_to, root_to, sem):
+    copies = [
+        pltpu.make_async_copy(src, dst, sem.at[i])
+        for i, (src, dst) in enumerate(((root_any, root_to), (stats_any, stats_to), (grad_any, grad_to)))
+    ]
+    for item in copies:
+        item.start()
+    for item in copies:
+        item.wait()
 
 
 def on_device(hidden_act, out_grad, layer_stats, resident_stats, slot_block, layer_refresh):
@@ -488,13 +507,14 @@
         pltpu.SemaphoreType.DMA((SEMS,)),
         pltpu.SemaphoreType.DMA((SEMS,)),
     ]
-    return pl.pallas_call(
+    shapes = (
+        jax.ShapeDtypeStruct((4, 1024), F32),
+        jax.ShapeDtypeStruct(layer_stats.shape, F32),
+        jax.ShapeDtypeStruct((1, BLK, BLK), F32),
+    )
+    made = pl.pallas_call(
         kernel,
-        out_shape=(
-            jax.ShapeDtypeStruct((4, 1024), F32),
-            jax.ShapeDtypeStruct(layer_stats.shape, F32),
-            jax.ShapeDtypeStruct((1, BLK, BLK), F32),
-        ),
+        out_shape=shapes,
         in_specs=[hbm] * 6,
         out_specs=(vmem, vmem, vmem),
         scratch_shapes=scratch,
@@ -506,6 +526,14 @@
         pltpu.with_memory_space_constraint(value, pltpu.HBM)
         for value in (hidden_act, out_grad, layer_stats, resident_stats, slot_block, layer_refresh)
     ])
+    anywhere = pl.BlockSpec(memory_space=pl.ANY)
+    return pl.pallas_call(
+        deliver,
+        out_shape=shapes,
+        in_specs=[vmem] * 3,
+        out_specs=(anywhere,) * 3,
+        scratch_shapes=[pltpu.SemaphoreType.DMA((3,))],
+    )(*[pltpu.with_memory_space_constraint(value, pltpu.VMEM) for value in made])
 
 
 def solution(mesh):

time: 58 us -> 56 us (0.966)
  local copies, waits for them, and re-layouts: 2.19 us -> 0 us
    unnamed x3 -> x0, local copies, waits for them, and re-layouts: 2.19 us -> none
    pallas_call x1 -> x2, Pallas kernels: 55.1 us -> 54.7 us  [the longest x1 53.7 us: on_device(): pl.pallas_call(kernel, out_shape=shapes, in_specs=[hbm] * 6, out_specs=(v...]
where the time goes in v4:
time: 56 us; the launch traced here: 55.4 us
  Pallas kernels  54.7 us (98%)
  between operations  0.64 us (1%)
    pallas_call x1, Pallas kernels, on_device(): pl.pallas_call(kernel, out_shape=shapes, in_specs=[hbm] * 6, out_specs=(v...  53.7 us

profile of v4, /device:TPU:1, one launch (start us, length us, event | category | flops | bytes accessed | tf_op | source)
XLA Modules:
  0.0 55.4 jit_solution(6678287550528183526)
XLA Ops:
  0.6 53.7 %shard_map.85 = (f32[4,1024]{1,0:T(4,128)S(1)}, f32[16,512]{1,0:T(8,128)S(1)}, f32[1,512,512]{2,1,0:T(8,128)S(1)}) custom-call(bf16[512,1024]{1,0:T(8,128)(2,1)} %hid_any.1, bf16[512,1024]{1,0:T(8,128)(2,1)} %og_any.1, f32[16,512]{1,0:T(8,128)} %stats_any.1, f32[4,512,512]{2,1,0:T(8,128)} %res_any.1, s32[1024]{0:T(1024)} %slots_any.1, s32[64]{0:T(128)} %refresh_any.1), custom_call_target="tpu_custom_call" | custom-call | flops 10000000000 | bytes 10000000 | tf_op jit(solution)/shard_map/pallas_call | solution.py:515
  54.4 1.0 %shard_map.86 = (f32[4,1024]{1,0:T(4,128)}, f32[16,512]{1,0:T(8,128)}, f32[1,512,512]{2,1,0:T(8,128)}) custom-call(f32[4,1024]{1,0:T(4,128)S(1)} %get-tuple-element.6.grad_any, f32[16,512]{1,0:T(8,128)S(1)} %get-tuple-element.7.stats_any, f32[1,512,512]{2,1,0:T(8,128)S(1)} %get-tuple-element.8.root_any), custom_call_target="tpu_custom_call" | custom-call | tf_op jit(solution)/shard_map/pallas_call | solution.py:530

commit v5 on v4

--- a/solution.py
+++ b/solution.py
@@ -16,7 +16,7 @@
 ROWS = 256
 NCH = 2
 PC = 4 // NCH
-LAG = 2
+LAG = 3
 HOOKS = (0, 8, 7, 0)
 SEMS = 100
 CUTS = (400, 408)
@@ -36,7 +36,7 @@
     grad_out, stats_out, root_out,
     hid, og, stats_in, res, slot_block, refresh,
     g_send, g_own, core_recv, s1a, s1b, p1a, p1b, a1, b1, p2a, p2b, r, p3, fin, fin_other,
-    tile, t_high, t_low, wide, pack, pack_recv,
+    tile, t_high, t_low, wide, corner, pack, pack_recv,
     m0, m0_h, m0_l, q_h, q_l, r_h, r_l, w_h, w_l, p_f, p_h, p_l,
     in_sem, send_sem, recv_sem,
 ):
@@ -184,9 +184,14 @@
         high[rows, :] = value_h
         low[rows, :] = value_l
 
-    def product(ah, al, bh, bl, rows):
+    def product(ah, al, bh, bl, i, rows):
+        cols = pl.ds(i * ROWS, BLK - i * ROWS)
         lead = ah[rows, :]
-        return dot(lead, bh[...]) + dot(lead, bl[...]) + dot(al[rows, :], bh[...])
+        value = dot(lead, bh[:, cols]) + dot(lead, bl[:, cols]) + dot(al[rows, :], bh[:, cols])
+        if i == 0:
+            corner[...] = value[:, ROWS:]
+            return value
+        return jnp.concatenate([corner[...].T, value], axis=1)
 
     def ident(i):
         r_ = lax.broadcasted_iota(jnp.int32, (ROWS, BLK), 0) + i * ROWS
@@ -194,29 +199,29 @@
         return (r_ == c_).astype(F32)
 
     def step1(i, rows):
-        square = product(m0_h, m0_l, m0_h, m0_l, rows)
+        square = product(m0_h, m0_l, m0_h, m0_l, i, rows)
         m = m0[rows, :]
         put(w_h, w_l, rows, (5.0 * m - square) * 0.25)
         put(q_h, q_l, rows, (25.0 * ident(i) - 10.0 * m + square) * 0.0625)
 
     def step2(i, rows):
-        put(r_h, r_l, rows, product(q_h, q_l, q_h, q_l, rows))
+        put(r_h, r_l, rows, product(q_h, q_l, q_h, q_l, i, rows))
 
     def step3(i, rows):
-        fifth = product(r_h, r_l, w_h, w_l, rows)
+        fifth = product(r_h, r_l, w_h, w_l, i, rows)
         factor = (5.0 * ident(i) - m0[rows, :]) * 0.25
         value = (5.0 * factor - fifth) * 0.25
         p_f[rows, :] = value
         put(p_h, p_l, rows, value)
 
     def step4(i, rows):
-        put(q_h, q_l, rows, product(p_h, p_l, p_h, p_l, rows))
+        put(q_h, q_l, rows, product(p_h, p_l, p_h, p_l, i, rows))
 
     def step5(i, rows):
-        put(w_h, w_l, rows, product(p_h, p_l, m0_h, m0_l, rows))
+        put(w_h, w_l, rows, product(p_h, p_l, m0_h, m0_l, i, rows))
 
     def step6(i, rows):
-        fifth = product(r_h, r_l, w_h, w_l, rows)
+        fifth = product(r_h, r_l, w_h, w_l, i, rows)
         root_out[0, rows, :] = (5.0 * p_f[rows, :] - fifth) * (0.25 * scale[0])
 
     def root_steps():
@@ -489,6 +494,7 @@
         pltpu.VMEM(square, BF16),
         pltpu.VMEM(square, BF16),
         pltpu.VMEM((128, BLK), F32),
+        pltpu.VMEM((HALF, HALF), F32),
         pltpu.VMEM((2 * HALF + 8, HALF), F32),
         pltpu.VMEM((2 * HALF + 8, HALF), F32),
         pltpu.VMEM(square, F32),

time: 56 us -> 55.5 us (level)
  the two profiles are of different devices: /device:TPU:1 before, /device:TPU:25 now
where the time goes in v5:
time: 55.5 us; the launch traced here: 55.4 us
  Pallas kernels  54.7 us (99%)
  between operations  0.64 us (1%)
    pallas_call x1, Pallas kernels, on_device(): pl.pallas_call(kernel, out_shape=shapes, in_specs=[hbm] * 6, out_specs=(v...  53.7 us

profile of v5, /device:TPU:25, one launch (start us, length us, event | category | flops | bytes accessed | tf_op | source)
XLA Modules:
  0.0 55.4 jit_solution(9137554033958307736)
XLA Ops:
  0.6 53.7 %shard_map.85 = (f32[4,1024]{1,0:T(4,128)S(1)}, f32[16,512]{1,0:T(8,128)S(1)}, f32[1,512,512]{2,1,0:T(8,128)S(1)}) custom-call(bf16[512,1024]{1,0:T(8,128)(2,1)} %hid_any.1, bf16[512,1024]{1,0:T(8,128)(2,1)} %og_any.1, f32[16,512]{1,0:T(8,128)} %stats_any.1, f32[4,512,512]{2,1,0:T(8,128)} %res_any.1, s32[1024]{0:T(1024)} %slots_any.1, s32[64]{0:T(128)} %refresh_any.1), custom_call_target="tpu_custom_call" | custom-call | flops 10000000000 | bytes 10000000 | tf_op jit(solution)/shard_map/pallas_call | solution.py:521
  54.4 1.0 %shard_map.86 = (f32[4,1024]{1,0:T(4,128)}, f32[16,512]{1,0:T(8,128)}, f32[1,512,512]{2,1,0:T(8,128)}) custom-call(f32[4,1024]{1,0:T(4,128)S(1)} %get-tuple-element.6.grad_any, f32[16,512]{1,0:T(8,128)S(1)} %get-tuple-element.7.stats_any, f32[1,512,512]{2,1,0:T(8,128)S(1)} %get-tuple-element.8.root_any), custom_call_target="tpu_custom_call" | custom-call | tf_op jit(solution)/shard_map/pallas_call | solution.py:536
